TPU v7x, 512 devices: a whole 4x4x16 slice. The times are simulated.
512 devices in a mesh: leaf: 128 (over z, x, core), sub: 4 (over y).
Axes of the slice: x: 4, y: 4, z: 16, core: 2. Of those that a mesh axis runs over, the one named last changes fastest.
Arguments:
- positions: float32 [3, 32, 131072], P(None, None, ('leaf', 'sub')), may hold values from 0 to 2, as said below
- charges: float32 [32, 131072], P(None, ('leaf', 'sub')), may hold values from -1.6 to 1.6
- m2l_ops: float32 [216, 3456], replicated, may hold values from -3 to 3
- near_list: int32 [131072, 27], P(('leaf', 'sub')), may hold values from -1 to 2047, as said below
- far_list: int32 [131072, 16], P(('leaf', 'sub')), may hold values from -1 to 2047, as said below
- send_slots: int32 [512, 128, 8], P(('leaf', 'sub')), may hold values from -1 to 255, as said below
Outputs:
- potential: float32 [32, 131072], P(None, ('leaf', 'sub'))
Inputs may be any that keep to these rules, and one draw needn't show every extreme that they name: `positions`: all 32 bodies of a leaf lie in one unit cube with integer corners, at least 0.01 inside its faces; leaves follow their cubes' Morton order. send_slots[g, p, c] is a leaf of device g (counted among its own 256) that g sends to the device of index p along leaf with g's index along sub, or -1. In each block [g, p] the live entries come first and are distinct; the block to g's own index is empty; a block to an index next to g's holds at most 8 live entries and one such block of every device holds exactly 8; any other block holds 1 to 3 and one of every device holds exactly 3. Entry 0 of row i is leaf i itself, as a row column. Every entry e >= 1024 names a live slot of send_slots, and every live slot sent to a device is named by some near_list entry of its leaves. Every entry e >= 1024 names a live slot of send_slots, and every live slot sent to a device is named by some far_list entry of its leaves.
All inputs are finite; a program needn't handle non-finite values.
Results may differ from a plain program's by a relative error of at most 0.0003.
Values sent between devices are 32-bit elements; how exact they have to be, the bound alone decides.
A program may use at most 192 MiB of HBM per device.

v0:
```python
import math

import jax
import jax.numpy as jnp
from jax import lax
from jax.sharding import PartitionSpec as P

NB = 32
ORDER = 6
NODES = 216
FAR = 16


SOFTENING = 0.0625
HIGHEST = lax.Precision.HIGHEST


def cheb_table():
    degrees = jnp.arange(ORDER, dtype=jnp.float32)
    angles = (2.0 * degrees[:, None] + 1.0) * degrees[None, :] * (math.pi / (2.0 * ORDER))
    weights = jnp.where(degrees[None, :] == 0.0, 1.0 / ORDER, 2.0 / ORDER)
    return jnp.cos(angles) * weights


def interp_factors(positions):
    scaled = 2.0 * (positions - jnp.floor(positions)) - 1.0
    table_values = cheb_table()
    factors = []
    for axis_id in range(3):
        coordinate = scaled[axis_id]
        polynomials = [jnp.ones_like(coordinate), coordinate]
        for degree in range(2, ORDER):
            polynomials.append(2.0 * coordinate * polynomials[-1] - polynomials[-2])
        stacked = jnp.stack(polynomials[:ORDER])
        factors.append(jnp.einsum("nk,kjl->njl", table_values, stacked, precision=HIGHEST))
    return factors


def to_moments(factors, charges):
    first_axis, second_axis, third_axis = factors
    pair_factor = second_axis[:, None] * third_axis[None, :]
    moments = jnp.einsum(
        "ajl,bcjl->abcl", first_axis * charges[None], pair_factor, precision=HIGHEST
    )
    return moments.reshape(NODES, -1)


def to_bodies(factors, expansions):
    first_axis, second_axis, third_axis = factors
    node_grid = expansions.reshape(ORDER, ORDER, ORDER, -1)
    inner_sum = jnp.einsum("cjl,abcl->abjl", third_axis, node_grid, precision=HIGHEST)
    second = jnp.einsum("bjl,abjl->ajl", second_axis, inner_sum, precision=HIGHEST)
    return jnp.sum(first_axis * second, axis=0)


def slot_term(target_pos, target_ids, source_pos, source_charge, source_ids):
    between = source_pos[:, :, None, :] - target_pos[:, None, :, :]
    distance_sq = jnp.sum(between * between, axis=0) + SOFTENING
    kernel = 1.0 / jnp.sqrt(distance_sq)
    same_body = jnp.eye(NB, dtype=jnp.bool_)[:, :, None] & (source_ids == target_ids)[None, None, :]
    kernel = jnp.where(same_body, 0.0, kernel)
    return jnp.sum(source_charge[:, None, :] * kernel, axis=0)


def per_device(positions, charges, m2l_ops, near_list, far_list, send_slots):
    own_count = positions.shape[2]
    sub_index = lax.axis_index("sub")
    bodies = jnp.concatenate([positions.reshape(3 * NB, own_count), charges], axis=0)
    own_factors = interp_factors(positions)
    payload = jnp.concatenate([bodies, to_moments(own_factors, charges)], axis=0)
    row_cells = lax.all_gather(payload, "sub", axis=1, tiled=True)
    slot_list = send_slots.reshape(-1)
    outgoing = jnp.take(payload, jnp.maximum(slot_list, 0), axis=1)
    outgoing = jnp.where((slot_list >= 0)[None, :], outgoing, 0.0)
    received = lax.all_to_all(outgoing, "leaf", split_axis=1, concat_axis=1, tiled=True)
    cell_table = jnp.concatenate([row_cells, received], axis=1)
    table_pos = cell_table[: 3 * NB].reshape(3, NB, -1)
    table_charge = cell_table[3 * NB : 4 * NB]
    table_moments = cell_table[4 * NB :]
    own_columns = sub_index * own_count + jnp.arange(own_count, dtype=jnp.int32)

    def near_step(running, column):
        is_valid = column >= 0
        safe_index = jnp.maximum(column, 0)
        source_pos = table_pos[:, :, safe_index]
        source_q = jnp.where(is_valid[None, :], table_charge[:, safe_index], 0.0)
        return (running + slot_term(positions, own_columns, source_pos, source_q, column), None)

    near_total, _ = lax.scan(near_step, jnp.zeros((NB, own_count), jnp.float32), near_list.T)
    far_valid = far_list >= 0
    gathered = jnp.take(table_moments, jnp.maximum(far_list, 0).T, axis=1)
    gathered = jnp.where(far_valid.T[None], gathered, 0.0)
    flat = gathered.reshape(NODES * FAR, own_count)
    expansions = jnp.dot(m2l_ops, flat, precision=HIGHEST, preferred_element_type=jnp.float32)
    return near_total + to_bodies(own_factors, expansions)


def solution(mesh):
    in_specs = (
        P(None, None, ("leaf", "sub")),
        P(None, ("leaf", "sub")),
        P(),
        P(("leaf", "sub"), None),
        P(("leaf", "sub"), None),
        P(("leaf", "sub"), None, None),
    )
    out_specs = P(None, ("leaf", "sub"))
    return jax.shard_map(
        per_device, mesh=mesh, in_specs=in_specs, out_specs=out_specs, check_vma=False
    )
```

profile of v0, /device:TPU:49, one launch (start us, length us, event | category | flops | bytes accessed | tf_op | source)
XLA Modules:
  0.0 514.8 jit_solution(11051750331902876024)
XLA Ops:
  23.5 12.4 %fusion.7 = f32[6,6,6,256]{0,2,1,3:T(8,128)} fusion(f32[6,32,256,1]{1,0,3,2:T(8,128)} %copy.74, f32[6,32,256]{1,0,2:T(8,128)} %copy.59, f32[6,32,256]{1,0,2:T(8,128)} %copy.57), kind=kOutput, calls=%fused_computation.26 | convolution fusion | flops 21528576 | bytes 811008 | tf_op jit(solution)/shard_map/ajl,bcjl->abcl/dot_general | solution.py:42
  36.0 5.9 %copy.62 = f32[6,6,6,256]{3,2,1,0:T(8,128)} copy(f32[6,6,6,256]{0,2,1,3:T(8,128)} %fusion.7) | data formatting | bytes 442368 | tf_op jit(solution)/shard_map/ajl,bcjl->abcl/transpose | solution.py:42
  45.4 4.8 gather_fusion.2
  53.1 19.8 %all-to-all-start = ((f32[344,128,8]{0,2,1:T(8,128)}), f32[344,128,8]{0,2,1:T(8,128)}, u32[]{:S(2)}, u32[]{:S(2)}) async-start(f32[344,128,8]{0,2,1:T(8,128)} %fusion.10), calls=%async_computation | async-start | bytes 3145728 | tf_op jit(solution)/shard_map/all_to_all | solution.py:75
  80.5 28.6 %all-gather.2.cloned.1.call-done = f32[344,1024]{0,1:T(8,128)} async-done(((f32[344,256]{0,1:T(8,128)}), f32[344,1024]{0,1:T(8,128)}) %all-gather.2.cloned.1.call-update) | async-done | bytes 1409040 | tf_op jit(solution)/shard_map/all_gather | solution.py:71
  109.1 41.1 %all-to-all-done = f32[344,128,8]{0,2,1:T(8,128)} async-done(((f32[344,128,8]{0,2,1:T(8,128)}), f32[344,128,8]{0,2,1:T(8,128)}, u32[]{:S(2)}, u32[]{:S(2)}) %all-to-all-start) | async-done | bytes 1409056 | tf_op jit(solution)/shard_map/all_to_all | solution.py:75
  154.9 4.5 copy.70
  161.9 293.1 %while.11 = (s32[]{:T(128)}, f32[32,256]{1,0:T(8,128)S(1)}, s32[27,256]{1,0:T(8,128)}, f32[32,2048]{0,1:T(8,128)}, f32[3,32,2048]{1,0,2:T(4,128)}, /*index=5*/f3...) while((s32[]{:T(128)}, f32[32,256]{1,0:T(8,128)S(1)}, s32[27,256]{1,0:T(8,128)}, ...), condition=%wide.region_3.4_spmd.clone, body=%wide.region_0.0_spmd.clone.sunk | while | flops 3427331 | bytes 3062903 | solution.py:89
  162.7 3.2 gather_fusion
  173.5 3.2 gather_fusion
  195.2 3.2 gather_fusion
  206.1 3.2 gather_fusion
  216.9 3.2 gather_fusion
  227.8 3.2 gather_fusion
  238.7 3.2 gather_fusion
  271.2 3.2 gather_fusion
  282.1 3.2 gather_fusion
  292.9 3.2 gather_fusion
  303.8 3.2 gather_fusion
  314.6 3.2 gather_fusion
  325.5 3.2 gather_fusion
  336.4 3.2 gather_fusion
  347.2 3.2 gather_fusion
  368.9 3.2 gather_fusion
  412.4 3.2 gather_fusion
  423.2 3.2 gather_fusion
  434.1 3.2 gather_fusion
  444.9 3.2 gather_fusion
  458.1 17.6 %gather_fusion.3 = f32[4096,216]{1,0:T(8,128)} fusion(f32[216,2048]{0,1:T(8,128)} %pad_maximum_fusion, s32[4096]{0:T(1024)S(1)} %copy-done.10), kind=kCustom, calls=%fused_computation.3 | custom fusion | bytes 7094272 | tf_op jit(solution)/shard_map/jit(_take)/gather | solution.py:91
  475.7 5.2 %copy.71 = f32[16,256,216]{1,0,2:T(8,128)} copy(f32[16,256,216]{2,1,0:T(8,128)} %bitcast.73) | data formatting | bytes 7077888 | tf_op jit(solution)/shard_map/jit(_take)/gather | solution.py:91
  486.4 5.0 copy.72
  491.3 14.3 %fusion.2 = f32[32,256,6]{0,2,1:T(8,128)} fusion(f32[32,256,6]{0,2,1:T(8,128)} %copy.88, f32[6,6,6,256]{2,1,0,3:T(8,128)} %copy.72, f32[6,32,256,1]{1,0,3,2:T(8,128)} %copy.75), kind=kOutput, calls=%fused_computation.16 | convolution fusion | flops 21774336 | bytes 811008 | tf_op jit(solution)/shard_map/cjl,abcl->abjl/dot_general | solution.py:51
  (408 shorter events, 275.9 us)
Async XLA Ops:
  6.5 476.8 %copy-start = (f32[216,3456]{1,0:T(8,128)S(1)}, f32[216,3456]{1,0:T(8,128)}, u32[]{:S(2)}) copy-start(f32[216,3456]{1,0:T(8,128)} %param.10) | copy-start | bytes 8957956
  13.6 6.9 %copy-start.9 = (f32[6,32,256]{2,1,0:T(8,128)}, f32[6,32,256]{2,1,0:T(8,128)S(1)}, u32[]{:S(2)}) copy-start(f32[6,32,256]{2,1,0:T(8,128)S(1)} %get-tuple-element.114) | copy-start | bytes 589828
  14.9 0.7 copy-start.7
  19.2 4.3 copy-start.3
  22.0 13.9 %copy-start.5 = (f32[6,32,256]{2,0,1:T(8,128)}, f32[6,32,256]{2,0,1:T(8,128)S(1)}, u32[]{:S(2)}) copy-start(f32[6,32,256]{2,0,1:T(8,128)S(1)} %fusion.18) | copy-start | bytes 589828
  36.0 7.8 %copy-start.2 = (f32[3,32,256]{2,1,0:T(8,128)S(1)}, f32[3,32,256]{2,1,0:T(8,128)}, u32[]{:S(2)}) copy-start(f32[3,32,256]{2,1,0:T(8,128)} %param.8) | copy-start | bytes 294916
  45.4 4.8 copy-start.1
  53.1 20.6 %copy-start.6 = (f32[6,32,256]{2,0,1:T(8,128)S(1)}, f32[6,32,256]{2,0,1:T(8,128)}, u32[]{:S(2)}) copy-start(f32[6,32,256]{2,0,1:T(8,128)} %copy-done.5) | copy-start | bytes 589828
  53.1 22.7 %copy-start.4 = (f32[6,32,256]{2,0,1:T(8,128)S(1)}, f32[6,32,256]{2,0,1:T(8,128)}, u32[]{:S(2)}) copy-start(f32[6,32,256]{2,0,1:T(8,128)} %copy-done.3) | copy-start | bytes 589828
  53.1 97.1 %all-to-all-start = ((f32[344,128,8]{0,2,1:T(8,128)}), f32[344,128,8]{0,2,1:T(8,128)}, u32[]{:S(2)}, u32[]{:S(2)}) async-start(f32[344,128,8]{0,2,1:T(8,128)} %fusion.10), calls=%async_computation | async-start | bytes 3145728 | tf_op jit(solution)/shard_map/all_to_all | solution.py:75
  73.0 36.1 %all-gather.2.cloned.1.call-start = ((), (), s32[]{:S(2)}) async-start(), calls=%async_computation.1 | async-start | bytes 1966080 | tf_op jit(solution)/shard_map/all_gather | solution.py:71
  455.0 3.0 copy-start.10
  475.7 5.2 %copy-start.11 = (pred[16,256]{1,0:T(8,128)(4,1)S(1)}, pred[16,256]{1,0:T(8,128)(4,1)}, u32[]{:S(2)}) copy-start(pred[16,256]{1,0:T(8,128)(4,1)} %compare_bitcast_fusion) | copy-start | bytes 12292
  475.7 5.2 %copy-start.12 = (pred[16,256]{1,0:T(8,128)(4,1)S(1)}, pred[16,256]{1,0:T(8,128)(4,1)}, u32[]{:S(2)}) copy-start(pred[16,256]{1,0:T(8,128)(4,1)} %compare_and_fusion) | copy-start | bytes 12292
  491.3 15.9 %copy-start.8 = (f32[6,32,256]{2,0,1:T(8,128)S(1)}, f32[6,32,256]{2,0,1:T(8,128)}, u32[]{:S(2)}) copy-start(f32[6,32,256]{2,0,1:T(8,128)} %copy-done.7) | copy-start | bytes 589828
Sparse Core Ops, SparseCore 0:
  75.9 33.1 all-gather.1
where the time goes:
time: 521 us; the launch traced here: 515 us
  local copies, waits for them, and re-layouts  221 us (42%)
  other arithmetic  155 us (30%)
  waiting for transfers between devices  70.3 us (13%)
  matrix products  33.1 us (6%)
  starting transfers between devices  20.1 us (4%)
  between operations  13.6 us (3%)
    gather x54, local copies, waits for them, and re-layouts, near_step(): source_pos = table_pos[:, :, safe_index]  108 us
    reduce_sum x27, other arithmetic, slot_term(): distance_sq = jnp.sum(between * between, axis=0) + SOFTENING  64.8 us
    gather x27, local copies, waits for them, and re-layouts, near_step(): source_q = jnp.where(is_valid[None, :], table_charge[:, safe_index], 0.0)  52.5 us
    reduce_sum x27, other arithmetic, slot_term(): return jnp.sum(source_charge[:, None, :] * kernel, axis=0)  41.1 us
    all_to_all x1, waiting for transfers between devices, per_device(): lax.all_to_all(outgoing, 'leaf', split_axis=1, concat_axis=1, tiled=True)  41.1 us
    all_gather x1, waiting for transfers between devices, per_device(): row_cells = lax.all_gather(payload, 'sub', axis=1, tiled=True)  28.6 us
    gather x2, local copies, waits for them, and re-layouts, per_device(): gathered = jnp.take(table_moments, jnp.maximum(far_list, 0).T, axis=1)  22.9 us
    all_to_all x1, starting transfers between devices, per_device(): lax.all_to_all(outgoing, 'leaf', split_axis=1, concat_axis=1, tiled=True)  19.8 us
  transfers between devices with their start and end apart: 2, of which 2 were waited for; matrix products, arithmetic and copies ran while one was open for 1% of the time, Pallas kernels for 0%

commit v1 on v0

v1 whole, which is shorter than its diff:
```python
import functools
import math

import jax
import jax.numpy as jnp
from jax import lax
from jax.experimental import pallas as pl
from jax.experimental.pallas import tpu as pltpu
from jax.sharding import PartitionSpec as P

NB = 32
ORDER = 6
NODES = 216
NEAR = 27
FAR = 16
CAP = 8
CAP_FAR = 3
SOFTENING = 0.0625
OWN = 256
PEERS = 128
ROW = 1024
RECV = PEERS * CAP_FAR
BESIDE = ROW + RECV
ZERO = BESIDE + 2 * CAP
TABLE = 1536
F32 = jnp.float32
BF16 = jnp.bfloat16


def factors_of(coordinate):
    x = 2.0 * (coordinate - jnp.floor(coordinate)) - 1.0
    polynomials = [None, x]
    for degree in range(2, ORDER):
        before = 1.0 if degree == 2 else polynomials[-2]
        polynomials.append(2.0 * x * polynomials[-1] - before)
    weight = lambda n, k: 2.0 / ORDER * math.cos(k * (2 * n + 1) * math.pi / 12)
    low, high = [], []
    for n in range(ORDER // 2):
        even = 1.0 / ORDER + weight(n, 4) * polynomials[4]
        if n != 1:
            even = even + weight(n, 2) * polynomials[2]
        odd = weight(n, 1) * x + weight(n, 3) * polynomials[3] + weight(n, 5) * polynomials[5]
        low.append(even + odd)
        high.append(even - odd)
    return low + high[::-1]


def fold_rows(parts):
    rows = lax.broadcasted_iota(jnp.int32, parts[0].shape, 0)
    for step in (4, 2, 1):
        first = (rows & step) == 0
        half = len(parts) // 2
        folded = []
        for n in range(half):
            p, q = parts[n], parts[n + half]
            kept = jnp.where(first, p, q)
            moved = jnp.where(first, q, p)
            if step == 4:
                folded.append(kept + pltpu.roll(moved, 4, 0))
            else:
                back = pltpu.roll(moved, step, 0)
                ahead = pltpu.roll(moved, 8 - step, 0)
                folded.append(kept + jnp.where(first, ahead, back))
        parts = folded
    return parts[0]


def moments_tile(table, start, cells, store):
    cells[...] = table[pl.ds(start, 128), :].T
    fx = factors_of(cells[0:32, :])
    fy = factors_of(cells[32:64, :])
    fz = factors_of(cells[64:96, :])
    charge = cells[96:128, :]
    parts = []
    node = 0
    for a in range(ORDER):
        qa = charge * fx[a]
        for b in range(ORDER):
            ab = qa * fy[b]
            for c in range(ORDER):
                abc = ab * fz[c]
                parts.append((abc[0:8] + abc[8:16]) + (abc[16:24] + abc[24:32]))
                node += 1
                if len(parts) == 8:
                    store(node - 8, fold_rows(parts))
                    parts = []


def local_kernel(
    near_idx, far_idx, rows, recv, beside, pos, charge, near_list, m2l,
    out, table, cells, moments, low_table, high_table,
    raw, near_cells, far_rows, far_flat, accum,
):
    table[0:ROW, :] = rows[...]
    table[ROW:BESIDE, :] = recv[...]
    table[BESIDE:ZERO, :] = beside[...]
    table[ZERO:TABLE, :] = jnp.zeros((TABLE - ZERO, 128), F32)
    moments[NODES:256, :] = jnp.zeros((256 - NODES, 128), F32)

    @pl.loop(0, TABLE // 128)
    def _(tile):
        start = pl.multiple_of(tile * 128, 128)

        def store(node, value):
            moments[node : node + 8, :] = value

        moments_tile(table, start, cells, store)
        low_table[pl.ds(start, 128), :] = moments[0:128, :].T
        high_table[pl.ds(start, 128), :] = moments[128:256, :].T

    out[...] = jnp.zeros((NB, OWN), F32)

    @pl.loop(0, NEAR)
    def _(k):
        for h in range(2):
            base = k * OWN + h * 128
            for i in range(128):
                raw[h, i : i + 1, :] = table[pl.ds(near_idx[base + i], 1), :]
            near_cells[h] = raw[h].T
            lanes = slice(h * 128, h * 128 + 128)
            tx, ty, tz = (pos[d * 32 : d * 32 + 32, lanes] for d in range(3))
            total = out[:, lanes]
            for a in range(NB):
                wide = lambda row: jnp.broadcast_to(near_cells[h, row : row + 1, :], (NB, 128))
                dx = wide(a) - tx
                dy = wide(32 + a) - ty
                dz = wide(64 + a) - tz
                square = (dx * dx + dy * dy) + (dz * dz + SOFTENING)
                total = total + wide(96 + a) * lax.rsqrt(square)
            out[:, lanes] = total

    @pl.loop(0, FAR)
    def _(k):
        for h in range(2):
            base = k * OWN + h * 128
            for i in range(128):
                cell = far_idx[base + i]
                far_rows[h, 0, i : i + 1, :] = low_table[pl.ds(cell, 1), :]
                far_rows[h, 1, i : i + 1, :] = high_table[pl.ds(cell, 1), :]
            flat = far_flat.at[h]
            flat[pl.ds(k, 128, stride=FAR), :] = far_rows[h, 0].T
            flat[pl.ds(k + 128 * FAR, NODES - 128, stride=FAR), :] = far_rows[h, 1].T[0 : NODES - 128]

    accum[...] = jnp.zeros((NODES, OWN), F32)
    for part in range(9):
        weights = m2l[:, part * 384 : part * 384 + 384]
        span = slice(part * 384, part * 384 + 384)
        values = jnp.concatenate([far_flat[0, span], far_flat[1, span]], axis=1)
        w_high = weights.astype(BF16)
        w_low = (weights - w_high.astype(F32)).astype(BF16)
        v_high = values.astype(BF16)
        v_low = (values - v_high.astype(F32)).astype(BF16)
        dot = functools.partial(jnp.dot, preferred_element_type=F32)
        accum[...] += dot(w_high, v_high) + (dot(w_high, v_low) + dot(w_low, v_high))

    own_first = lax.axis_index("sub") * OWN
    for h in range(2):
        lanes = slice(h * 128, h * 128 + 128)
        fx, fy, fz = (factors_of(pos[d * 32 : d * 32 + 32, lanes]) for d in range(3))
        wide = lambda row: jnp.broadcast_to(accum[row : row + 1, lanes], (NB, 128))
        total = out[:, lanes]
        for a in range(ORDER):
            for b in range(ORDER):
                inner = wide(a * 36 + b * 6) * fz[0]
                for c in range(1, ORDER):
                    inner = inner + wide(a * 36 + b * 6 + c) * fz[c]
                second = inner * fy[b] if b == 0 else second + inner * fy[b]
            total = total + second * fx[a]
        own = own_first + h * 128 + lax.broadcasted_iota(jnp.int32, (1, 128), 1)
        itself = (near_list[:, lanes] == own).astype(F32)
        count = jnp.sum(itself, axis=0, keepdims=True)
        out[:, lanes] = total - (4.0 * count) * charge[:, lanes]


def local_call(near_idx, far_idx, rows, recv, beside, pos, charge, near_list, m2l):
    vmem = pl.BlockSpec(memory_space=pltpu.VMEM)
    smem = pl.BlockSpec(memory_space=pltpu.SMEM)
    return pl.pallas_call(
        local_kernel,
        out_shape=jax.ShapeDtypeStruct((NB, OWN), F32),
        in_specs=[smem, smem] + [vmem] * 7,
        out_specs=vmem,
        scratch_shapes=[
            pltpu.VMEM((TABLE, 128), F32),
            pltpu.VMEM((128, 128), F32),
            pltpu.VMEM((256, 128), F32),
            pltpu.VMEM((TABLE, 128), F32),
            pltpu.VMEM((TABLE, 128), F32),
            pltpu.VMEM((2, 128, 128), F32),
            pltpu.VMEM((2, 128, 128), F32),
            pltpu.VMEM((2, 2, 128, 128), F32),
            pltpu.VMEM((2, NODES * FAR, 128), F32),
            pltpu.VMEM((NODES, OWN), F32),
        ],
        compiler_params=pltpu.CompilerParams(vmem_limit_bytes=40 * 2**20),
    )(near_idx, far_idx, rows, recv, beside, pos, charge, near_list, m2l)


def table_rows(entries, row_index):
    away = entries - ROW
    peer, slot = away >> 3, away & 7
    far = ROW + peer * CAP_FAR + jnp.minimum(slot, CAP_FAR - 1)
    left = BESIDE + slot
    remote = jnp.where(
        peer == row_index - 1, left, jnp.where(peer == row_index + 1, left + CAP, far)
    )
    return jnp.where(entries < 0, ZERO, jnp.where(entries < ROW, entries, remote))


def per_device(positions, charges, m2l_ops, near_list, far_list, send_slots):
    row_index = lax.axis_index("leaf")
    pos = positions.reshape(3 * NB, OWN)
    bodies = jnp.concatenate([pos, charges], axis=0).T
    rows = lax.all_gather(bodies, "sub", axis=0, tiled=True)
    slots = jnp.maximum(send_slots[0], 0)
    outgoing = jnp.take(bodies, slots[:, :CAP_FAR].reshape(-1), axis=0)
    recv = lax.all_to_all(
        outgoing.reshape(PEERS, CAP_FAR * 128), "leaf", split_axis=0, concat_axis=0, tiled=True
    ).reshape(RECV, 128)
    to_right = jnp.take(bodies, slots[jnp.minimum(row_index + 1, PEERS - 1)], axis=0)
    to_left = jnp.take(bodies, slots[jnp.maximum(row_index - 1, 0)], axis=0)
    ring = [(p, (p + 1) % PEERS) for p in range(PEERS)]
    from_left = lax.ppermute(to_right, "leaf", ring)
    from_right = lax.ppermute(to_left, "leaf", [(q, p) for p, q in ring])
    beside = jnp.concatenate([from_left, from_right], axis=0)
    near_t, far_t = near_list.T, far_list.T
    near_idx = table_rows(near_t, row_index).reshape(-1)
    far_idx = table_rows(far_t, row_index).reshape(-1)
    return local_call(near_idx, far_idx, rows, recv, beside, pos, charges, near_t, m2l_ops)


def solution(mesh):
    in_specs = (
        P(None, None, ("leaf", "sub")),
        P(None, ("leaf", "sub")),
        P(),
        P(("leaf", "sub"), None),
        P(("leaf", "sub"), None),
        P(("leaf", "sub"), None, None),
    )
    out_specs = P(None, ("leaf", "sub"))
    return jax.shard_map(
        per_device, mesh=mesh, in_specs=in_specs, out_specs=out_specs, check_vma=False
    )
```

time: 521 us -> 99.2 us (0.19)
  the two profiles are of different devices: /device:TPU:49 before, /device:TPU:8 now
where the time goes in v1:
time: 99.2 us; the launch traced here: 98.5 us
  Pallas kernels  39.7 us (40%)
  starting transfers between devices  28.9 us (29%)
  blocking collectives  13.7 us (14%)
  local copies, waits for them, and re-layouts  12 us (12%)
  other arithmetic  3.96 us (4%)
    pallas_call x1, Pallas kernels, local_call(): pl.pallas_call(local_kernel, out_shape=jax.ShapeDtypeStruct((NB, OWN), F3...  39.7 us
    all_to_all x1, starting transfers between devices, per_device(): lax.all_to_all(outgoing.reshape(PEERS, CAP_FAR * 128), 'leaf', split_axis...  20.2 us
    all_gather x1, blocking collectives, per_device(): rows = lax.all_gather(bodies, 'sub', axis=0, tiled=True)  13.7 us
    ppermute x1, starting transfers between devices, per_device(): from_right = lax.ppermute(to_left, 'leaf', [(q, p) for p, q in ring])  6.78 us
    unnamed x13, local copies, waits for them, and re-layouts  3.73 us
    gather x3, local copies, waits for them, and re-layouts, per_device(): outgoing = jnp.take(bodies, slots[:, :CAP_FAR].reshape(-1), axis=0)  2.89 us
  transfers between devices with their start and end apart: 3, of which 0 were waited for; matrix products, arithmetic and copies ran while one was open for 5% of the time, Pallas kernels for 0%

profile of v1, /device:TPU:8, one launch (start us, length us, event | category | flops | bytes accessed | tf_op | source)
XLA Modules:
  0.0 98.5 jit_solution(6701493510795191059)
XLA Ops:
  0.0 0.7 broadcast_maximum_fusion
  0.7 0.9 maximum_bitcast_fusion
  1.6 0.1 copy.20
  1.7 0.1 copy.19
  1.8 0.0 copy-start
  1.9 0.2 reshape.87
  2.1 1.1 %gather_fusion = f32[384,128]{1,0:T(8,128)S(1)} fusion(f32[256,128]{1,0:T(8,128)S(1)} %copy.20, s32[1024]{0:T(1024)S(1)} %pad_clamp_fusion.2), kind=kCustom, calls=%fused_computation.2 | custom fusion | bytes 394752 | tf_op jit(solution)/shard_map/jit(_take)/gather | solution.py:216
  3.2 0.7 gather.10
  4.0 1.1 %copy.21 = f32[128,1,384]{0,2,1:T(8,128)S(1)} copy(f32[128,1,384]{2,0,1:T(8,128)} %gather.10) | data formatting | bytes 393216 | tf_op jit(solution)/shard_map/jit(_take)/gather | solution.py:216
  5.0 0.7 bitcast_select_fusion
  5.7 1.7 %copy.22 = f32[128,1,384]{2,1,0:T(1,128)} copy(f32[128,1,384]{0,2,1:T(8,128)} %bitcast_select_fusion) | data formatting | bytes 393216 | tf_op jit(solution)/shard_map/jit(_take)/select_n | solution.py:216
  7.5 20.2 %all-to-all-start = ((f32[128,1,384]{2,1,0:T(1,128)}), f32[128,1,384]{2,1,0:T(1,128)}, u32[]{:S(2)}, u32[]{:S(2)}) async-start(f32[128,1,384]{2,1,0:T(1,128)} %copy.22), calls=%async_computation | async-start | bytes 393216 | tf_op jit(solution)/shard_map/all_to_all | solution.py:217
  27.7 0.2 dynamic-slice_reduce_fusion.1
  28.0 0.6 gather_fusion.2
  28.5 0.1 broadcast_select_fusion
  28.6 6.8 %collective-permute-start.1 = (f32[8,128]{1,0:T(8,128)S(1)}, f32[8,128]{1,0:T(8,128)S(1)}, u32[]{:S(2)}, u32[]{:S(2)}) collective-permute-start(f32[8,128]{1,0:T(8,128)S(1)} %broadcast_select_fusion), channel_id=1, source_target_pairs={{4,0},{8,4},{12,8},{16,12},{20,16},{24,20},{28,24},{32,28},{36,32}... | collective-permute-start | bytes 12296 | tf_op jit(solution)/shard_map/ppermute | solution.py:224
  35.4 0.6 gather_fusion.1
  36.0 0.1 broadcast_select_fusion.1
  36.1 1.9 %collective-permute-start = (f32[8,128]{1,0:T(8,128)S(1)}, f32[8,128]{1,0:T(8,128)}, u32[]{:S(2)}, u32[]{:S(2)}) collective-permute-start(f32[8,128]{1,0:T(8,128)S(1)} %broadcast_select_fusion.1), channel_id=1, source_target_pairs={{0,4},{4,8},{8,12},{12,16},{16,20},{20,24},{24,28},{28,32},{32,36}... | collective-permute-start | bytes 12296 | tf_op jit(solution)/shard_map/ppermute | solution.py:223
  38.0 0.7 fusion.2
  38.8 13.7 %all_gather.3 = f32[1024,128]{0,1:T(8,128)} all-gather(f32[256,128]{0,1:T(8,128)S(1)} %maximum_bitcast_fusion), channel_id=1, replica_groups=mesh['leaf'=128,'sub'=4] {'sub'}, dimensions={0}, use_global_device_ids=true | all-gather | bytes 655360 | tf_op jit(solution)/shard_map/all_gather | solution.py:214
  52.5 0.6 reshape.84.near_idx
  53.1 0.6 copy.26
  53.7 1.2 %copy.25.rows = f32[1024,128]{1,0:T(8,128)S(1)} copy(f32[1024,128]{0,1:T(8,128)} %all_gather.3) | data formatting | bytes 1048576 | tf_op jit(solution)/shard_map/all_gather | solution.py:214
  55.0 0.0 collective-permute-done.1
  55.0 0.0 collective-permute-done
  55.0 0.7 pad_maximum_fusion.beside
  55.7 0.9 copy-done.1
  56.6 0.8 copy-done.3
  57.3 0.7 copy-done.4
  58.1 0.7 copy-done.5
  58.8 39.7 %shard_map.64 = f32[32,256]{1,0:T(8,128)} custom-call(s32[6912]{0:T(1024)S(1)} %copy-done.4, s32[4096]{0:T(1024)S(1)} %bitcast.25, f32[1024,128]{1,0:T(8,128)S(1)} %copy.25.rows, f32[384,128]{1,0:T(8,128)} %bitcast.6.recv, f32[16,128]{1,0:T(8,128)S(1)} %pad_maximum_fusion.beside, f32[96,256]{1,0:T(8,128)S(1)} %bitcast.23, f32[32,256]{1,0:T(8,128)S(1)} %copy-done.3, ...), custom_call_target="tpu_custom_call" | custom-call | tf_op jit(solution)/shard_map/pallas_call | solution.py:178
  (20 shorter events, 0.1 us)
Async XLA Ops:
  0.0 38.7 %copy-start.2 = (s32[256,27]{0,1:T(8,128)S(1)}, s32[256,27]{0,1:T(8,128)}, u32[]{:S(2)}) copy-start(s32[256,27]{0,1:T(8,128)} %param.11) | copy-start | bytes 82948
  1.8 53.8 %copy-start = (f32[216,3456]{1,0:T(8,128)S(1)}, f32[216,3456]{1,0:T(8,128)}, u32[]{:S(2)}) copy-start(f32[216,3456]{1,0:T(8,128)} %m2l.1) | copy-start | bytes 8957956
  7.5 48.2 %all-to-all-start = ((f32[128,1,384]{2,1,0:T(1,128)}), f32[128,1,384]{2,1,0:T(1,128)}, u32[]{:S(2)}, u32[]{:S(2)}) async-start(f32[128,1,384]{2,1,0:T(1,128)} %copy.22), calls=%async_computation | async-start | bytes 393216 | tf_op jit(solution)/shard_map/all_to_all | solution.py:217
  28.6 26.4 %collective-permute-start.1 = (f32[8,128]{1,0:T(8,128)S(1)}, f32[8,128]{1,0:T(8,128)S(1)}, u32[]{:S(2)}, u32[]{:S(2)}) collective-permute-start(f32[8,128]{1,0:T(8,128)S(1)} %broadcast_select_fusion), channel_id=1, source_target_pairs={{4,0},{8,4},{12,8},{16,12},{20,16},{24,20},{28,24},{32,28},{36,32}... | collective-permute-start | bytes 12296 | tf_op jit(solution)/shard_map/ppermute | solution.py:224
  36.1 18.9 %collective-permute-start = (f32[8,128]{1,0:T(8,128)S(1)}, f32[8,128]{1,0:T(8,128)}, u32[]{:S(2)}, u32[]{:S(2)}) collective-permute-start(f32[8,128]{1,0:T(8,128)S(1)} %broadcast_select_fusion.1), channel_id=1, source_target_pairs={{0,4},{4,8},{8,12},{12,16},{16,20},{20,24},{24,28},{28,32},{32,36}... | collective-permute-start | bytes 12296 | tf_op jit(solution)/shard_map/ppermute | solution.py:223
  55.7 0.9 copy-start.1
  56.6 0.8 copy-start.3
  57.3 0.7 copy-start.4
  58.1 0.7 copy-start.5

commit v2 on v1

v2 whole, which is shorter than its diff:
```python
import functools
import math

import jax
import jax.numpy as jnp
from jax import lax
from jax.experimental import pallas as pl
from jax.experimental.pallas import tpu as pltpu
from jax.sharding import PartitionSpec as P

NB = 32
ORDER = 6
NODES = 216
NEAR = 27
FAR = 16
CAP = 8
CAP_FAR = 3
SOFTENING = 0.0625
OWN = 256
PEERS = 128
ROW = 1024
RECV = PEERS * CAP_FAR
BESIDE = ROW + RECV
ZERO = BESIDE + 2 * CAP
TABLE = 1536
F32 = jnp.float32
BF16 = jnp.bfloat16
MESH = pl.DeviceIdType.MESH


def factors_of(coordinate):
    x = 2.0 * (coordinate - jnp.floor(coordinate)) - 1.0
    polynomials = [None, x]
    for degree in range(2, ORDER):
        before = 1.0 if degree == 2 else polynomials[-2]
        polynomials.append(2.0 * x * polynomials[-1] - before)
    weight = lambda n, k: 2.0 / ORDER * math.cos(k * (2 * n + 1) * math.pi / 12)
    low, high = [], []
    for n in range(ORDER // 2):
        even = 1.0 / ORDER + weight(n, 4) * polynomials[4]
        if n != 1:
            even = even + weight(n, 2) * polynomials[2]
        odd = weight(n, 1) * x + weight(n, 3) * polynomials[3] + weight(n, 5) * polynomials[5]
        low.append(even + odd)
        high.append(even - odd)
    return low + high[::-1]


def fold_rows(parts):
    rows = lax.broadcasted_iota(jnp.int32, parts[0].shape, 0)
    for step in (4, 2, 1):
        first = (rows & step) == 0
        half = len(parts) // 2
        folded = []
        for n in range(half):
            p, q = parts[n], parts[n + half]
            kept = jnp.where(first, p, q)
            moved = jnp.where(first, q, p)
            if step == 4:
                folded.append(kept + pltpu.roll(moved, 4, 0))
            else:
                back = pltpu.roll(moved, step, 0)
                ahead = pltpu.roll(moved, 8 - step, 0)
                folded.append(kept + jnp.where(first, ahead, back))
        parts = folded
    return parts[0]


def table_rows(entries, row_index):
    away = entries - ROW
    peer, slot = away >> 3, away & 7
    far = ROW + peer * CAP_FAR + jnp.minimum(slot, CAP_FAR - 1)
    left = BESIDE + slot
    remote = jnp.where(
        peer == row_index - 1, left, jnp.where(peer == row_index + 1, left + CAP, far)
    )
    return jnp.where(entries < 0, ZERO, jnp.where(entries < ROW, entries, remote))


def split(value):
    high = value.astype(BF16)
    return high, (value - high.astype(F32)).astype(BF16)


def spread_tile(cell, spread, start):
    once, twice, thrice = (pltpu.roll(cell, n * 32, 1) for n in (1, 2, 3))
    which = lax.broadcasted_iota(jnp.int32, (64, 128), 1) >> 5
    odd, upper = (which & 1) == 1, (which & 2) == 2
    p, q = jnp.where(odd, once, cell), jnp.where(odd, thrice, twice)
    u, v = jnp.where(odd, cell, thrice), jnp.where(odd, twice, once)
    x = jnp.where(upper, q, p) - 1.0
    y = jnp.where(upper, v, u) - 1.0
    z = jnp.where(upper, p, q) - 1.0
    values = (-2.0 * x, -2.0 * y, -2.0 * z, x * x + y * y + z * z, jnp.where(upper, u, v))
    for f, value in enumerate(values):
        spread[pl.ds(start * 8 + f, 64, stride=8), :] = value


def moments_tile(table, spread, cells, moments, start):
    cells[...] = table[pl.ds(start, 128), :].T
    fx = factors_of(cells[0:32, :])
    fy = factors_of(cells[32:64, :])
    fz = factors_of(cells[64:96, :])
    charge = cells[96:128, :]
    parts = []
    node = 0
    for a in range(ORDER):
        qa = charge * fx[a]
        for b in range(ORDER):
            ab = qa * fy[b]
            for c in range(ORDER):
                abc = ab * fz[c]
                parts.append((abc[0:8] + abc[8:16]) + (abc[16:24] + abc[24:32]))
                node += 1
                if len(parts) == 8:
                    moments[node - 8 : node, :] = fold_rows(parts)
                    parts = []
    spread[pl.ds(start * 8 + 5, 128, stride=8), :] = moments[0:128, :].T
    spread[pl.ds(start * 8 + 6, 128, stride=8), :] = moments[128:256, :].T


def potential_kernel(
    pos, charge, near_list, far_list, slots, m2l_hbm,
    out,
    own, outgoing, beside_out, table, recv, beside, m2l,
    near_rows, far_rows, near_idx, far_idx,
    cells, moments, spread, near_sums, far_cells, op_table, operators, accum, expanded,
    local_sems, row_send, row_recv, leaf_send, leaf_recv, beside_send, beside_recv,
):
    row = lax.axis_index("leaf")
    sub = lax.axis_index("sub")
    own_first = sub * OWN
    barrier = pltpu.get_barrier_semaphore()

    @pl.loop(1, PEERS)
    def _(step):
        peer = lax.rem(row + step, PEERS)
        pl.semaphore_signal(barrier, inc=1, device_id=(peer, sub), device_id_type=MESH)

    for step in (1, 2, 3):
        pl.semaphore_signal(
            barrier, inc=1, device_id=(row, lax.rem(sub + step, 4)), device_id_type=MESH
        )

    fetch = pltpu.make_async_copy(m2l_hbm, m2l, local_sems.at[0])
    fetch.start()

    for h in range(2):
        lanes = slice(h * 128, h * 128 + 128)
        own[lanes, :] = jnp.concatenate([pos[:, lanes], charge[:, lanes]], axis=0).T

    @pl.loop(0, PEERS // 8)
    def _(block):
        for u in range(8):
            peer = block * 8 + u
            for c in range(CAP_FAR):
                slot = jnp.maximum(slots[c, peer], 0)
                outgoing[peer * CAP_FAR + c] = own[pl.ds(slot, 1), :]

    left, right = lax.rem(row + PEERS - 1, PEERS), lax.rem(row + 1, PEERS)
    for side, peer in enumerate((left, right)):
        for c in range(CAP):
            slot = jnp.maximum(slots[c, peer], 0)
            beside_out[side, c : c + 1, :] = own[pl.ds(slot, 1), :]

    pl.semaphore_wait(barrier, PEERS - 1 + 3)

    def row_copy(step):
        return pltpu.make_async_remote_copy(
            src_ref=own,
            dst_ref=table.at[pl.ds(pl.multiple_of(own_first, OWN), OWN)],
            send_sem=row_send.at[step - 1],
            recv_sem=row_recv.at[step - 1],
            device_id=(row, lax.rem(sub + step, 4)),
            device_id_type=MESH,
        )

    def leaf_copy(peer):
        return pltpu.make_async_remote_copy(
            src_ref=outgoing.at[pl.ds(peer * CAP_FAR, CAP_FAR)],
            dst_ref=recv.at[pl.ds(row * CAP_FAR, CAP_FAR)],
            send_sem=leaf_send,
            recv_sem=leaf_recv,
            device_id=(peer, sub),
            device_id_type=MESH,
        )

    def beside_copy(side, peer):
        return pltpu.make_async_remote_copy(
            src_ref=beside_out.at[side],
            dst_ref=beside.at[1 - side],
            send_sem=beside_send.at[side],
            recv_sem=beside_recv.at[1 - side],
            device_id=(peer, sub),
            device_id_type=MESH,
        )

    for step in (1, 3, 2):
        row_copy(step).start()

    @pl.loop(1, PEERS // 2)
    def _(step):
        leaf_copy(lax.rem(row + step, PEERS)).start()
        leaf_copy(lax.rem(row + PEERS - step, PEERS)).start()

    leaf_copy(lax.rem(row + PEERS // 2, PEERS)).start()
    beside_copy(0, left).start()
    beside_copy(1, right).start()

    near_rows[...] = table_rows(near_list[...], row)
    far_rows[...] = table_rows(far_list[...], row)
    near_move = pltpu.make_async_copy(near_rows, near_idx, local_sems.at[1])
    far_move = pltpu.make_async_copy(far_rows, far_idx, local_sems.at[2])
    near_move.start()
    far_move.start()

    fetch.wait()
    moments[NODES:256, :] = jnp.zeros((256 - NODES, 128), F32)
    op_table[:, NODES * FAR :, :] = jnp.zeros((2, (256 - NODES) * FAR, 128), F32)

    @pl.loop(0, NODES * FAR // 128)
    def _(tile):
        start = pl.multiple_of(tile * 128, 128)
        op_table[0, pl.ds(start, 128), :] = m2l[0:128, pl.ds(start, 128)].T
        rest = m2l[128:NODES, pl.ds(start, 128)].T
        op_table[1, pl.ds(start, 128), 0 : NODES - 128] = rest
        op_table[1, pl.ds(start, 128), NODES - 128 :] = jnp.zeros((128, 256 - NODES), F32)

    @pl.loop(0, FAR)
    def _(k):
        for half in range(2):
            plane = op_table.at[half]
            high, low = split(plane[pl.ds(k, 256, stride=FAR), :])
            operators[k, 0:256, half * 128 : half * 128 + 128] = high
            operators[k, 256:512, half * 128 : half * 128 + 128] = low

    def build(start):
        for part in range(2):
            at = pl.multiple_of(start + part * 64, 64)
            spread_tile(table[pl.ds(at, 64), :], spread, at)
        moments_tile(table, spread, cells, moments, start)

    table[pl.ds(pl.multiple_of(own_first, OWN), OWN), :] = own[...]
    for step in range(4):
        if step:
            row_copy(step).wait_recv()
        first = lax.rem(sub + 4 - step, 4) * OWN

        @pl.loop(0, 2)
        def _(tile):
            build(pl.multiple_of(first + tile * 128, 128))

    recv[pl.ds(row * CAP_FAR, CAP_FAR)] = jnp.zeros((CAP_FAR, 1, 128), F32)
    beside_copy(1, left).wait_recv()
    beside_copy(0, right).wait_recv()
    everything = pl.ds(0, (PEERS - 1) * CAP_FAR)
    pltpu.make_async_copy(recv.at[everything], recv.at[everything], leaf_recv).wait()
    blocks = table.reshape(TABLE // 8, 8, 128)

    @pl.loop(0, RECV // 8)
    def _(block):
        for u in range(8):
            blocks[ROW // 8 + block, u : u + 1, :] = recv[block * 8 + u]

    for side in range(2):
        table[BESIDE + side * CAP : BESIDE + side * CAP + CAP, :] = beside[side]
    table[ZERO:TABLE, :] = jnp.zeros((TABLE - ZERO, 128), F32)

    @pl.loop(ROW // 128, TABLE // 128)
    def _(tile):
        build(pl.multiple_of(tile * 128, 128))

    near_move.wait()
    far_move.wait()
    lane = lax.broadcasted_iota(jnp.int32, (8, 128), 1)
    group = lane >> 5
    target = group * 8 + lax.broadcasted_iota(jnp.int32, (8, 128), 0)
    spread_cells = spread.reshape(TABLE, 8, 128)

    @pl.loop(0, OWN // 8)
    def _(block):
        for u in range(8):
            i = block * 8 + u
            mine = jnp.broadcast_to(own[pl.ds(i, 1), :], (8, 128))
            tx, ty, tz = (
                jnp.take_along_axis(mine, target + 32 * d, axis=1, mode="promise_in_bounds") - 1.0
                for d in range(3)
            )
            level = (tx * tx + ty * ty) + (tz * tz + SOFTENING)
            sums = [None, None]
            for k in range(NEAR):
                cell = near_idx[k, i]
                wide = lambda f: jnp.broadcast_to(spread_cells[cell, f : f + 1, :], (8, 128))
                square = (wide(0) * tx + wide(1) * ty) + (wide(2) * tz + (wide(3) + level))
                term = wide(4) * lax.rsqrt(square)
                sums[k % 2] = term if k < 2 else sums[k % 2] + term
            near_sums[pl.ds(i, 8, stride=OWN), :] = sums[0] + sums[1]
            for k in range(FAR):
                far_cells[k, block, 2 * u : 2 * u + 2, :] = spread_cells[far_idx[k, i], 5:7, :]

    far_flat = far_cells.reshape(FAR * OWN * 2, 128)
    dot = functools.partial(jnp.dot, preferred_element_type=F32)
    accum[...] = jnp.zeros((OWN, 256), F32)

    @pl.loop(0, FAR // 2)
    def _(pair):
        total = accum[...]
        for n in range(2):
            k = pair * 2 + n
            values = jnp.concatenate(
                [far_flat[pl.ds(k * OWN * 2 + half, OWN, stride=2), :] for half in range(2)], axis=1
            )
            high, low = split(values)
            total = total + dot(jnp.concatenate([high, high], axis=1), operators[k])
            total = total + dot(low, operators[k, 0:256])
        accum[...] = total

    for h in range(2):
        for t in range(2):
            expanded[t * 128 : t * 128 + 128, h * 128 : h * 128 + 128] = accum[
                h * 128 : h * 128 + 128, t * 128 : t * 128 + 128
            ].T

    ones = (lax.broadcasted_iota(jnp.int32, (8, 128), 0) == group).astype(BF16)
    across = (((1,), (1,)), ((), ()))
    for s in range(8):
        high, low = split(near_sums[s * OWN : s * OWN + OWN, :])
        both = lax.dot_general(ones, high, across, preferred_element_type=F32) + lax.dot_general(
            ones, low, across, preferred_element_type=F32
        )
        for g in range(4):
            out[g * 8 + s : g * 8 + s + 1, :] = both[g : g + 1, :]

    for h in range(2):
        lanes = slice(h * 128, h * 128 + 128)
        fx, fy, fz = (factors_of(pos[d * 32 : d * 32 + 32, lanes]) for d in range(3))
        wide = lambda row: jnp.broadcast_to(expanded[row : row + 1, lanes], (NB, 128))
        total = out[:, lanes]
        for a in range(ORDER):
            for b in range(ORDER):
                inner = wide(a * 36 + b * 6) * fz[0]
                for c in range(1, ORDER):
                    inner = inner + wide(a * 36 + b * 6 + c) * fz[c]
                second = inner * fy[b] if b == 0 else second + inner * fy[b]
            total = total + second * fx[a]
        mine = own_first + h * 128 + lax.broadcasted_iota(jnp.int32, (1, 128), 1)
        itself = (near_list[:, lanes] == mine).astype(F32)
        count = jnp.sum(itself, axis=0, keepdims=True)
        out[:, lanes] = total - (4.0 * count) * charge[:, lanes]

    for step in (1, 2, 3):
        row_copy(step).wait_send()
    beside_copy(0, left).wait_send()
    beside_copy(1, right).wait_send()
    pltpu.make_async_copy(outgoing.at[everything], outgoing.at[everything], leaf_send).wait()


def potential_call(pos, charge, near_list, far_list, slots, m2l):
    vmem = pl.BlockSpec(memory_space=pltpu.VMEM)
    smem = pl.BlockSpec(memory_space=pltpu.SMEM)
    dma = pltpu.SemaphoreType.DMA
    return pl.pallas_call(
        potential_kernel,
        out_shape=jax.ShapeDtypeStruct((NB, OWN), F32),
        in_specs=[vmem, vmem, vmem, vmem, smem, pl.BlockSpec(memory_space=pl.ANY)],
        out_specs=vmem,
        scratch_shapes=[
            pltpu.VMEM((OWN, 128), F32),
            pltpu.VMEM((RECV, 1, 128), F32),
            pltpu.VMEM((2, CAP, 128), F32),
            pltpu.VMEM((TABLE, 128), F32),
            pltpu.VMEM((RECV, 1, 128), F32),
            pltpu.VMEM((2, CAP, 128), F32),
            pltpu.VMEM((NODES, NODES * FAR), F32),
            pltpu.VMEM((NEAR, OWN), jnp.int32),
            pltpu.VMEM((FAR, OWN), jnp.int32),
            pltpu.SMEM((NEAR, OWN), jnp.int32),
            pltpu.SMEM((FAR, OWN), jnp.int32),
            pltpu.VMEM((128, 128), F32),
            pltpu.VMEM((256, 128), F32),
            pltpu.VMEM((TABLE * 8, 128), F32),
            pltpu.VMEM((8 * OWN, 128), F32),
            pltpu.VMEM((FAR, OWN // 8, 16, 128), F32),
            pltpu.VMEM((2, 256 * FAR, 128), F32),
            pltpu.VMEM((FAR, 512, 256), BF16),
            pltpu.VMEM((OWN, 256), F32),
            pltpu.VMEM((256, OWN), F32),
            dma((3,)),
            dma((3,)),
            dma((3,)),
            dma,
            dma,
            dma((2,)),
            dma((2,)),
        ],
        compiler_params=pltpu.CompilerParams(
            collective_id=0, has_side_effects=True, vmem_limit_bytes=48 * 2**20
        ),
    )(pos, charge, near_list, far_list, slots, m2l)


def per_device(positions, charges, m2l_ops, near_list, far_list, send_slots):
    pos = positions.reshape(3 * NB, OWN)
    return potential_call(pos, charges, near_list.T, far_list.T, send_slots[0].T, m2l_ops)


def solution(mesh):
    in_specs = (
        P(None, None, ("leaf", "sub")),
        P(None, ("leaf", "sub")),
        P(),
        P(("leaf", "sub"), None),
        P(("leaf", "sub"), None),
        P(("leaf", "sub"), None, None),
    )
    out_specs = P(None, ("leaf", "sub"))
    return jax.shard_map(
        per_device, mesh=mesh, in_specs=in_specs, out_specs=out_specs, check_vma=False
    )
```

time: 99.2 us -> 63.4 us (0.64)
  the two profiles are of different devices: /device:TPU:8 before, /device:TPU:1 now
where the time goes in v2:
time: 63.4 us; the launch traced here: 63 us
  Pallas kernels  56.7 us (89%)
  local copies, waits for them, and re-layouts  6.27 us (10%)
    pallas_call x1, Pallas kernels, potential_call(): pl.pallas_call(potential_kernel, out_shape=jax.ShapeDtypeStruct((NB, OWN)...  56.7 us
    unnamed x13, local copies, waits for them, and re-layouts  6.27 us

profile of v2, /device:TPU:1, one launch (start us, length us, event | category | flops | bytes accessed | tf_op | source)
XLA Modules:
  0.0 63.0 jit_solution(775294476690554003)
XLA Ops:
  0.0 0.0 copy-start
  0.0 1.8 %copy-done = f32[216,3456]{1,0:T(8,128)S(1)} copy-done((f32[216,3456]{1,0:T(8,128)S(1)}, f32[216,3456]{1,0:T(8,128)}, u32[]{:S(2)}) %copy-start) | copy-done | bytes 2986008
  1.8 0.0 copy-start.1
  1.8 0.9 %copy-done.1 = f32[3,32,256]{2,1,0:T(8,128)S(1)} copy-done((f32[3,32,256]{2,1,0:T(8,128)S(1)}, f32[3,32,256]{2,1,0:T(8,128)}, u32[]{:S(2)}) %copy-start.1) | copy-done | bytes 98328
  2.7 0.0 copy-start.2
  2.7 0.8 %copy-done.2 = f32[32,256]{1,0:T(8,128)S(1)} copy-done((f32[32,256]{1,0:T(8,128)S(1)}, f32[32,256]{1,0:T(8,128)}, u32[]{:S(2)}) %copy-start.2) | copy-done | bytes 32792
  3.5 0.0 copy-start.3
  3.5 0.8 %copy-done.3 = s32[256,27]{0,1:T(8,128)S(1)} copy-done((s32[256,27]{0,1:T(8,128)S(1)}, s32[256,27]{0,1:T(8,128)}, u32[]{:S(2)}) %copy-start.3) | copy-done | bytes 27672
  4.3 0.0 copy-start.4
  4.3 0.7 %copy-done.4 = s32[256,16]{0,1:T(8,128)S(1)} copy-done((s32[256,16]{0,1:T(8,128)S(1)}, s32[256,16]{0,1:T(8,128)}, u32[]{:S(2)}) %copy-start.4) | copy-done | bytes 16408
  5.0 0.0 copy-start.5
  5.0 0.7 %copy-done.5 = s32[1,128,8]{1,2,0:T(8,128)S(1)} copy-done((s32[1,128,8]{1,2,0:T(8,128)S(1)}, s32[1,128,8]{1,2,0:T(8,128)}, u32[]{:S(2)}) %copy-start.5) | copy-done | bytes 4120
  5.7 56.7 %shard_map.64 = f32[32,256]{1,0:T(8,128)S(1)} custom-call(f32[96,256]{1,0:T(8,128)S(1)} %bitcast.6, f32[32,256]{1,0:T(8,128)S(1)} %copy-done.2, s32[27,256]{1,0:T(8,128)S(1)} %bitcast.7, s32[16,256]{1,0:T(8,128)S(1)} %bitcast.8, s32[8,128]{1,0:T(8,128)S(1)} %bitcast.9, f32[216,3456]{1,0:T(8,128)S(1)} %copy-done), custom_call_target="tpu_custom_call" | custom-call | tf_op jit(solution)/shard_map/pallas_call | solution.py:362
  62.4 0.6 copy.8
Async XLA Ops:
  0.0 1.8 %copy-start = (f32[216,3456]{1,0:T(8,128)S(1)}, f32[216,3456]{1,0:T(8,128)}, u32[]{:S(2)}) copy-start(f32[216,3456]{1,0:T(8,128)} %m2l_hbm.1) | copy-start | bytes 8957956
  1.8 0.9 %copy-start.1 = (f32[3,32,256]{2,1,0:T(8,128)S(1)}, f32[3,32,256]{2,1,0:T(8,128)}, u32[]{:S(2)}) copy-start(f32[3,32,256]{2,1,0:T(8,128)} %param.6) | copy-start | bytes 294916
  2.7 0.8 %copy-start.2 = (f32[32,256]{1,0:T(8,128)S(1)}, f32[32,256]{1,0:T(8,128)}, u32[]{:S(2)}) copy-start(f32[32,256]{1,0:T(8,128)} %charge.1) | copy-start | bytes 98308
  3.5 0.8 %copy-start.3 = (s32[256,27]{0,1:T(8,128)S(1)}, s32[256,27]{0,1:T(8,128)}, u32[]{:S(2)}) copy-start(s32[256,27]{0,1:T(8,128)} %param.9) | copy-start | bytes 82948
  4.3 0.7 %copy-start.4 = (s32[256,16]{0,1:T(8,128)S(1)}, s32[256,16]{0,1:T(8,128)}, u32[]{:S(2)}) copy-start(s32[256,16]{0,1:T(8,128)} %param.10) | copy-start | bytes 49156
  5.0 0.7 %copy-start.5 = (s32[1,128,8]{1,2,0:T(8,128)S(1)}, s32[1,128,8]{1,2,0:T(8,128)}, u32[]{:S(2)}) copy-start(s32[1,128,8]{1,2,0:T(8,128)} %param.11) | copy-start | bytes 12292

commit v3 on v2

--- a/solution.py
+++ b/solution.py
@@ -18,6 +18,8 @@
 SOFTENING = 0.0625
 OWN = 256
 PEERS = 128
+PLANE = 8
+LINE = 16
 ROW = 1024
 RECV = PEERS * CAP_FAR
 BESIDE = ROW + RECV
@@ -120,50 +122,77 @@
 
 
 def potential_kernel(
-    pos, charge, near_list, far_list, slots, m2l_hbm,
+    pos_hbm, charge_hbm, near_hbm, far_hbm, slots_hbm, m2l_hbm,
     out,
-    own, outgoing, beside_out, table, recv, beside, m2l,
+    bodies, near_list, far_list, slots, own, outgoing, stage, beside_out, table, recv, beside, m2l,
     near_rows, far_rows, near_idx, far_idx,
     cells, moments, spread, near_sums, far_cells, op_table, operators, accum, expanded,
-    local_sems, row_send, row_recv, leaf_send, leaf_recv, beside_send, beside_recv,
+    local_sems, list_sems, row_send, row_recv, plane_send, plane_recv, line_send, line_recv,
+    beside_send, beside_recv,
 ):
     row = lax.axis_index("leaf")
     sub = lax.axis_index("sub")
+    line, plane = row // PLANE, row % PLANE
     own_first = sub * OWN
+    left, right = lax.rem(row + PEERS - 1, PEERS), lax.rem(row + 1, PEERS)
+
+    def in_plane(step):
+        return line * PLANE + lax.rem(plane + step, PLANE)
+
+    def on_line(step):
+        return lax.rem(line + step, LINE) * PLANE + plane
+
     barrier = pltpu.get_barrier_semaphore()
 
-    @pl.loop(1, PEERS)
-    def _(step):
-        peer = lax.rem(row + step, PEERS)
-        pl.semaphore_signal(barrier, inc=1, device_id=(peer, sub), device_id_type=MESH)
-
+    def greet(peer, peer_sub):
+        pl.semaphore_signal(barrier, inc=1, device_id=(peer, peer_sub), device_id_type=MESH)
+
+    for step in range(1, PLANE):
+        greet(in_plane(step), sub)
+    for step in range(1, LINE):
+        greet(on_line(step), sub)
     for step in (1, 2, 3):
-        pl.semaphore_signal(
-            barrier, inc=1, device_id=(row, lax.rem(sub + step, 4)), device_id_type=MESH
-        )
-
-    fetch = pltpu.make_async_copy(m2l_hbm, m2l, local_sems.at[0])
-    fetch.start()
+        greet(row, lax.rem(sub + step, 4))
+    greet(left, sub)
+    greet(right, sub)
+
+    fetches = [
+        pltpu.make_async_copy(source, target, local_sems.at[n])
+        for n, (source, target) in enumerate(
+            [
+                (pos_hbm, bodies.at[0:96]),
+                (charge_hbm, bodies.at[96:128]),
+                (slots_hbm, slots),
+                (near_hbm, near_list),
+                (far_hbm, far_list),
+                (m2l_hbm, m2l),
+            ]
+        )
+    ]
+    for fetch in fetches:
+        fetch.start()
+    fetches[0].wait()
+    fetches[1].wait()
 
     for h in range(2):
         lanes = slice(h * 128, h * 128 + 128)
-        own[lanes, :] = jnp.concatenate([pos[:, lanes], charge[:, lanes]], axis=0).T
-
-    @pl.loop(0, PEERS // 8)
-    def _(block):
-        for u in range(8):
-            peer = block * 8 + u
+        own[lanes, :] = bodies[:, lanes].T
+
+    fetches[2].wait()
+
+    @pl.loop(0, LINE)
+    def _(far_line):
+        for peer_plane in range(PLANE):
             for c in range(CAP_FAR):
-                slot = jnp.maximum(slots[c, peer], 0)
-                outgoing[peer * CAP_FAR + c] = own[pl.ds(slot, 1), :]
-
-    left, right = lax.rem(row + PEERS - 1, PEERS), lax.rem(row + 1, PEERS)
+                slot = jnp.maximum(slots[c, far_line * PLANE + peer_plane], 0)
+                outgoing[peer_plane, far_line, c] = own[pl.ds(slot, 1), :]
+
     for side, peer in enumerate((left, right)):
         for c in range(CAP):
             slot = jnp.maximum(slots[c, peer], 0)
             beside_out[side, c : c + 1, :] = own[pl.ds(slot, 1), :]
 
-    pl.semaphore_wait(barrier, PEERS - 1 + 3)
+    pl.semaphore_wait(barrier, PLANE - 1 + LINE - 1 + 3 + 2)
 
     def row_copy(step):
         return pltpu.make_async_remote_copy(
@@ -175,15 +204,31 @@
             device_id_type=MESH,
         )
 
-    def leaf_copy(peer):
+    def plane_copy(step):
+        peer = in_plane(step)
         return pltpu.make_async_remote_copy(
-            src_ref=outgoing.at[pl.ds(peer * CAP_FAR, CAP_FAR)],
-            dst_ref=recv.at[pl.ds(row * CAP_FAR, CAP_FAR)],
-            send_sem=leaf_send,
-            recv_sem=leaf_recv,
+            src_ref=outgoing.at[peer % PLANE],
+            dst_ref=stage.at[plane],
+            send_sem=plane_send,
+            recv_sem=plane_recv,
             device_id=(peer, sub),
             device_id_type=MESH,
         )
+
+    def line_copy(step):
+        peer = on_line(step)
+        return pltpu.make_async_remote_copy(
+            src_ref=stage.at[:, peer // PLANE],
+            dst_ref=recv.at[line],
+            send_sem=line_send,
+            recv_sem=line_recv,
+            device_id=(peer, sub),
+            device_id_type=MESH,
+        )
+
+    def wait_all(blocks, count, sem):
+        some = blocks.at[pl.ds(0, count)]
+        pltpu.make_async_copy(some, some, sem).wait()
 
     def beside_copy(side, peer):
         return pltpu.make_async_remote_copy(
@@ -195,27 +240,59 @@
             device_id_type=MESH,
         )
 
+    for step in range(1, PLANE):
+        plane_copy(step).start()
     for step in (1, 3, 2):
         row_copy(step).start()
-
-    @pl.loop(1, PEERS // 2)
-    def _(step):
-        leaf_copy(lax.rem(row + step, PEERS)).start()
-        leaf_copy(lax.rem(row + PEERS - step, PEERS)).start()
-
-    leaf_copy(lax.rem(row + PEERS // 2, PEERS)).start()
     beside_copy(0, left).start()
     beside_copy(1, right).start()
 
-    near_rows[...] = table_rows(near_list[...], row)
-    far_rows[...] = table_rows(far_list[...], row)
-    near_move = pltpu.make_async_copy(near_rows, near_idx, local_sems.at[1])
-    far_move = pltpu.make_async_copy(far_rows, far_idx, local_sems.at[2])
-    near_move.start()
-    far_move.start()
-
-    fetch.wait()
+    @pl.loop(0, LINE)
+    def _(far_line):
+        for c in range(CAP_FAR):
+            stage[plane, far_line, c] = outgoing[plane, far_line, c]
+
+    fetches[3].wait()
+    fetches[4].wait()
+    for entries, rows in ((near_list, near_rows), (far_list, far_rows)):
+        named = table_rows(entries[...], row)
+        for k in range(rows.shape[0]):
+            rows[k] = named[k : k + 1, :]
+    moves = [
+        pltpu.make_async_copy(
+            rows.at[k, 0], flat.at[pl.ds(k * OWN, OWN)], list_sems.at[first + k]
+        )
+        for rows, flat, first, count in ((near_rows, near_idx, 0, NEAR), (far_rows, far_idx, NEAR, FAR))
+        for k in range(count)
+    ]
+    for move in moves:
+        move.start()
+
+    def build(start):
+        for part in range(2):
+            at = pl.multiple_of(start + part * 64, 64)
+            spread_tile(table[pl.ds(at, 64), :], spread, at)
+        moments_tile(table, spread, cells, moments, start)
+
+    def build_row(first):
+        @pl.loop(0, 2)
+        def _(tile):
+            build(pl.multiple_of(first + tile * 128, 128))
+
     moments[NODES:256, :] = jnp.zeros((256 - NODES, 128), F32)
+    table[pl.ds(pl.multiple_of(own_first, OWN), OWN), :] = own[...]
+    build_row(own_first)
+
+    wait_all(stage, PLANE - 1, plane_recv)
+    for step in range(1, LINE // 2):
+        line_copy(step).start()
+        line_copy(LINE - step).start()
+    line_copy(LINE // 2).start()
+    for peer_plane in range(PLANE):
+        for c in range(CAP_FAR):
+            recv[line, peer_plane, c] = stage[peer_plane, line, c]
+
+    fetches[5].wait()
     op_table[:, NODES * FAR :, :] = jnp.zeros((2, (256 - NODES) * FAR, 128), F32)
 
     @pl.loop(0, NODES * FAR // 128)
@@ -234,33 +311,21 @@
             operators[k, 0:256, half * 128 : half * 128 + 128] = high
             operators[k, 256:512, half * 128 : half * 128 + 128] = low
 
-    def build(start):
-        for part in range(2):
-            at = pl.multiple_of(start + part * 64, 64)
-            spread_tile(table[pl.ds(at, 64), :], spread, at)
-        moments_tile(table, spread, cells, moments, start)
-
-    table[pl.ds(pl.multiple_of(own_first, OWN), OWN), :] = own[...]
-    for step in range(4):
-        if step:
-            row_copy(step).wait_recv()
-        first = lax.rem(sub + 4 - step, 4) * OWN
-
-        @pl.loop(0, 2)
-        def _(tile):
-            build(pl.multiple_of(first + tile * 128, 128))
-
-    recv[pl.ds(row * CAP_FAR, CAP_FAR)] = jnp.zeros((CAP_FAR, 1, 128), F32)
+    for step in (1, 3, 2):
+        row_copy(step).wait_recv()
+        build_row(lax.rem(sub + 4 - step, 4) * OWN)
+
     beside_copy(1, left).wait_recv()
     beside_copy(0, right).wait_recv()
-    everything = pl.ds(0, (PEERS - 1) * CAP_FAR)
-    pltpu.make_async_copy(recv.at[everything], recv.at[everything], leaf_recv).wait()
+    wait_all(recv, LINE - 1, line_recv)
     blocks = table.reshape(TABLE // 8, 8, 128)
 
-    @pl.loop(0, RECV // 8)
-    def _(block):
-        for u in range(8):
-            blocks[ROW // 8 + block, u : u + 1, :] = recv[block * 8 + u]
+    @pl.loop(0, LINE)
+    def _(far_line):
+        for n in range(PLANE * CAP_FAR):
+            blocks[ROW // 8 + far_line * PLANE * CAP_FAR // 8 + n // 8, n % 8 : n % 8 + 1, :] = recv[
+                far_line, n // CAP_FAR, n % CAP_FAR
+            ]
 
     for side in range(2):
         table[BESIDE + side * CAP : BESIDE + side * CAP + CAP, :] = beside[side]
@@ -270,50 +335,55 @@
     def _(tile):
         build(pl.multiple_of(tile * 128, 128))
 
-    near_move.wait()
-    far_move.wait()
+    for move in moves:
+        move.wait()
     lane = lax.broadcasted_iota(jnp.int32, (8, 128), 1)
     group = lane >> 5
     target = group * 8 + lax.broadcasted_iota(jnp.int32, (8, 128), 0)
     spread_cells = spread.reshape(TABLE, 8, 128)
 
-    @pl.loop(0, OWN // 8)
+    def near_leaf(i):
+        mine = jnp.broadcast_to(own[pl.ds(i, 1), :], (8, 128))
+        tx, ty, tz = (
+            jnp.take_along_axis(mine, target + 32 * d, axis=1, mode="promise_in_bounds") - 1.0
+            for d in range(3)
+        )
+        level = (tx * tx + ty * ty) + (tz * tz + SOFTENING)
+        sums = [None, None]
+        for k in range(NEAR):
+            cell = near_idx[k * OWN + i]
+            wide = lambda f: jnp.broadcast_to(spread_cells[cell, f : f + 1, :], (8, 128))
+            square = (wide(0) * tx + wide(1) * ty) + (wide(2) * tz + (wide(3) + level))
+            term = wide(4) * lax.rsqrt(square)
+            sums[k % 2] = term if k < 2 else sums[k % 2] + term
+        near_sums[pl.ds(i, 8, stride=OWN), :] = sums[0] + sums[1]
+
+    @pl.loop(0, OWN // 16)
     def _(block):
         for u in range(8):
-            i = block * 8 + u
-            mine = jnp.broadcast_to(own[pl.ds(i, 1), :], (8, 128))
-            tx, ty, tz = (
-                jnp.take_along_axis(mine, target + 32 * d, axis=1, mode="promise_in_bounds") - 1.0
-                for d in range(3)
-            )
-            level = (tx * tx + ty * ty) + (tz * tz + SOFTENING)
-            sums = [None, None]
-            for k in range(NEAR):
-                cell = near_idx[k, i]
-                wide = lambda f: jnp.broadcast_to(spread_cells[cell, f : f + 1, :], (8, 128))
-                square = (wide(0) * tx + wide(1) * ty) + (wide(2) * tz + (wide(3) + level))
-                term = wide(4) * lax.rsqrt(square)
-                sums[k % 2] = term if k < 2 else sums[k % 2] + term
-            near_sums[pl.ds(i, 8, stride=OWN), :] = sums[0] + sums[1]
-            for k in range(FAR):
-                far_cells[k, block, 2 * u : 2 * u + 2, :] = spread_cells[far_idx[k, i], 5:7, :]
+            near_leaf(block * 8 + u)
+            for half in range(2):
+                for k in range(FAR):
+                    cell = far_idx[k * OWN + half * (OWN // 2) + block * 8 + u]
+                    far_cells[k, half * (OWN // 16) + block, 2 * u : 2 * u + 2, :] = spread_cells[
+                        cell, 5:7, :
+                    ]
 
     far_flat = far_cells.reshape(FAR * OWN * 2, 128)
     dot = functools.partial(jnp.dot, preferred_element_type=F32)
     accum[...] = jnp.zeros((OWN, 256), F32)
 
-    @pl.loop(0, FAR // 2)
-    def _(pair):
-        total = accum[...]
-        for n in range(2):
-            k = pair * 2 + n
-            values = jnp.concatenate(
-                [far_flat[pl.ds(k * OWN * 2 + half, OWN, stride=2), :] for half in range(2)], axis=1
-            )
-            high, low = split(values)
-            total = total + dot(jnp.concatenate([high, high], axis=1), operators[k])
-            total = total + dot(low, operators[k, 0:256])
-        accum[...] = total
+    @pl.loop(0, FAR)
+    def _(k):
+        values = jnp.concatenate(
+            [far_flat[pl.ds(k * OWN * 2 + half, OWN, stride=2), :] for half in range(2)], axis=1
+        )
+        high, low = split(values)
+        accum[...] += dot(jnp.concatenate([high, high], axis=1), operators[k]) + dot(
+            low, operators[k, 0:256]
+        )
+        for u in range(8):
+            near_leaf(OWN // 2 + k * 8 + u)
 
     for h in range(2):
         for t in range(2):
@@ -333,7 +403,7 @@
 
     for h in range(2):
         lanes = slice(h * 128, h * 128 + 128)
-        fx, fy, fz = (factors_of(pos[d * 32 : d * 32 + 32, lanes]) for d in range(3))
+        fx, fy, fz = (factors_of(bodies[d * 32 : d * 32 + 32, lanes]) for d in range(3))
         wide = lambda row: jnp.broadcast_to(expanded[row : row + 1, lanes], (NB, 128))
         total = out[:, lanes]
         for a in range(ORDER):
@@ -346,36 +416,41 @@
         mine = own_first + h * 128 + lax.broadcasted_iota(jnp.int32, (1, 128), 1)
         itself = (near_list[:, lanes] == mine).astype(F32)
         count = jnp.sum(itself, axis=0, keepdims=True)
-        out[:, lanes] = total - (4.0 * count) * charge[:, lanes]
+        out[:, lanes] = total - (4.0 * count) * bodies[96:128, lanes]
 
     for step in (1, 2, 3):
         row_copy(step).wait_send()
     beside_copy(0, left).wait_send()
     beside_copy(1, right).wait_send()
-    pltpu.make_async_copy(outgoing.at[everything], outgoing.at[everything], leaf_send).wait()
+    wait_all(outgoing, PLANE - 1, plane_send)
+    wait_all(recv, LINE - 1, line_send)
 
 
 def potential_call(pos, charge, near_list, far_list, slots, m2l):
     vmem = pl.BlockSpec(memory_space=pltpu.VMEM)
-    smem = pl.BlockSpec(memory_space=pltpu.SMEM)
     dma = pltpu.SemaphoreType.DMA
     return pl.pallas_call(
         potential_kernel,
         out_shape=jax.ShapeDtypeStruct((NB, OWN), F32),
-        in_specs=[vmem, vmem, vmem, vmem, smem, pl.BlockSpec(memory_space=pl.ANY)],
+        in_specs=[pl.BlockSpec(memory_space=pl.ANY)] * 6,
         out_specs=vmem,
         scratch_shapes=[
+            pltpu.VMEM((128, OWN), F32),
+            pltpu.VMEM((NEAR, OWN), jnp.int32),
+            pltpu.VMEM((FAR, OWN), jnp.int32),
+            pltpu.SMEM((CAP, PEERS), jnp.int32),
             pltpu.VMEM((OWN, 128), F32),
-            pltpu.VMEM((RECV, 1, 128), F32),
+            pltpu.VMEM((PLANE, LINE, CAP_FAR, 1, 128), F32),
+            pltpu.VMEM((PLANE, LINE, CAP_FAR, 1, 128), F32),
             pltpu.VMEM((2, CAP, 128), F32),
             pltpu.VMEM((TABLE, 128), F32),
-            pltpu.VMEM((RECV, 1, 128), F32),
+            pltpu.VMEM((LINE, PLANE, CAP_FAR, 1, 128), F32),
             pltpu.VMEM((2, CAP, 128), F32),
             pltpu.VMEM((NODES, NODES * FAR), F32),
-            pltpu.VMEM((NEAR, OWN), jnp.int32),
-            pltpu.VMEM((FAR, OWN), jnp.int32),
-            pltpu.SMEM((NEAR, OWN), jnp.int32),
-            pltpu.SMEM((FAR, OWN), jnp.int32),
+            pltpu.VMEM((NEAR, 1, OWN), jnp.int32),
+            pltpu.VMEM((FAR, 1, OWN), jnp.int32),
+            pltpu.SMEM((NEAR * OWN,), jnp.int32),
+            pltpu.SMEM((FAR * OWN,), jnp.int32),
             pltpu.VMEM((128, 128), F32),
             pltpu.VMEM((256, 128), F32),
             pltpu.VMEM((TABLE * 8, 128), F32),
@@ -385,16 +460,19 @@
             pltpu.VMEM((FAR, 512, 256), BF16),
             pltpu.VMEM((OWN, 256), F32),
             pltpu.VMEM((256, OWN), F32),
+            dma((6,)),
+            dma((NEAR + FAR,)),
             dma((3,)),
             dma((3,)),
-            dma((3,)),
+            dma,
+            dma,
             dma,
             dma,
             dma((2,)),
             dma((2,)),
         ],
         compiler_params=pltpu.CompilerParams(
-            collective_id=0, has_side_effects=True, vmem_limit_bytes=48 * 2**20
+            collective_id=0, has_side_effects=True, vmem_limit_bytes=60 * 2**20
         ),
     )(pos, charge, near_list, far_list, slots, m2l)
 

time: 63.4 us -> 60.1 us (0.948)
  the two profiles are of different devices: /device:TPU:1 before, /device:TPU:8 now
where the time goes in v3:
time: 60.1 us; the launch traced here: 59.9 us
  Pallas kernels  58.6 us (98%)
  local copies, waits for them, and re-layouts  1.38 us (2%)
    pallas_call x1, Pallas kernels, potential_call(): pl.pallas_call(potential_kernel, out_shape=jax.ShapeDtypeStruct((NB, OWN)...  58.6 us
    unnamed x1, local copies, waits for them, and re-layouts  1.38 us

profile of v3, /device:TPU:8, one launch (start us, length us, event | category | flops | bytes accessed | tf_op | source)
XLA Modules:
  0.0 59.9 jit_solution(15251068042628593437)
XLA Ops:
  0.0 58.6 %shard_map.64 = f32[32,256]{1,0:T(8,128)} custom-call(f32[96,256]{1,0:T(8,128)} %bitcast.6, f32[32,256]{1,0:T(8,128)} %charge_hbm.1, s32[27,256]{1,0:T(8,128)} %bitcast.7, s32[16,256]{1,0:T(8,128)} %bitcast.8, s32[8,128]{1,0:T(8,128)} %bitcast.9, f32[216,3456]{1,0:T(8,128)} %m2l_hbm.1), custom_call_target="tpu_custom_call" | custom-call | tf_op jit(solution)/shard_map/pallas_call | solution.py:432
  58.6 1.4 %copy.8 = f32[32,256]{1,0:T(8,128)} copy(f32[32,256]{1,0:T(8,128)} %shard_map.64) | data formatting | bytes 65536

commit v4 on v3

--- a/solution.py
+++ b/solution.py
@@ -295,7 +295,7 @@
     fetches[5].wait()
     op_table[:, NODES * FAR :, :] = jnp.zeros((2, (256 - NODES) * FAR, 128), F32)
 
-    @pl.loop(0, NODES * FAR // 128)
+    @pl.loop(0, NODES * FAR // 128, unroll=3)
     def _(tile):
         start = pl.multiple_of(tile * 128, 128)
         op_table[0, pl.ds(start, 128), :] = m2l[0:128, pl.ds(start, 128)].T
@@ -303,7 +303,7 @@
         op_table[1, pl.ds(start, 128), 0 : NODES - 128] = rest
         op_table[1, pl.ds(start, 128), NODES - 128 :] = jnp.zeros((128, 256 - NODES), F32)
 
-    @pl.loop(0, FAR)
+    @pl.loop(0, FAR, unroll=2)
     def _(k):
         for half in range(2):
             plane = op_table.at[half]
@@ -358,32 +358,31 @@
             sums[k % 2] = term if k < 2 else sums[k % 2] + term
         near_sums[pl.ds(i, 8, stride=OWN), :] = sums[0] + sums[1]
 
-    @pl.loop(0, OWN // 16)
+    @pl.loop(0, OWN // 8, unroll=2)
     def _(block):
         for u in range(8):
-            near_leaf(block * 8 + u)
-            for half in range(2):
-                for k in range(FAR):
-                    cell = far_idx[k * OWN + half * (OWN // 2) + block * 8 + u]
-                    far_cells[k, half * (OWN // 16) + block, 2 * u : 2 * u + 2, :] = spread_cells[
-                        cell, 5:7, :
-                    ]
+            i = block * 8 + u
+            near_leaf(i)
+            for k in range(FAR):
+                cell = far_idx[k * OWN + i]
+                far_cells[k, block, 2 * u : 2 * u + 2, :] = spread_cells[cell, 5:7, :]
 
     far_flat = far_cells.reshape(FAR * OWN * 2, 128)
     dot = functools.partial(jnp.dot, preferred_element_type=F32)
     accum[...] = jnp.zeros((OWN, 256), F32)
 
-    @pl.loop(0, FAR)
-    def _(k):
-        values = jnp.concatenate(
-            [far_flat[pl.ds(k * OWN * 2 + half, OWN, stride=2), :] for half in range(2)], axis=1
-        )
-        high, low = split(values)
-        accum[...] += dot(jnp.concatenate([high, high], axis=1), operators[k]) + dot(
-            low, operators[k, 0:256]
-        )
-        for u in range(8):
-            near_leaf(OWN // 2 + k * 8 + u)
+    @pl.loop(0, FAR // 2)
+    def _(pair):
+        total = accum[...]
+        for n in range(2):
+            k = pair * 2 + n
+            values = jnp.concatenate(
+                [far_flat[pl.ds(k * OWN * 2 + half, OWN, stride=2), :] for half in range(2)], axis=1
+            )
+            high, low = split(values)
+            total = total + dot(jnp.concatenate([high, high], axis=1), operators[k])
+            total = total + dot(low, operators[k, 0:256])
+        accum[...] = total
 
     for h in range(2):
         for t in range(2):

time: 60.1 us -> 57.7 us (0.960)
  Pallas kernels: 58.6 us -> 56.2 us
    pallas_call x1, Pallas kernels: 58.6 us -> 56.2 us  [potential_call(): pl.pallas_call(potential_kernel, out_shape=jax.ShapeDtypeStruct((NB, OWN)...]
where the time goes in v4:
time: 57.7 us; the launch traced here: 57.5 us
  Pallas kernels  56.2 us (97%)
  local copies, waits for them, and re-layouts  1.38 us (2%)
    pallas_call x1, Pallas kernels, potential_call(): pl.pallas_call(potential_kernel, out_shape=jax.ShapeDtypeStruct((NB, OWN)...  56.2 us
    unnamed x1, local copies, waits for them, and re-layouts  1.38 us

profile of v4, /device:TPU:8, one launch (start us, length us, event | category | flops | bytes accessed | tf_op | source)
XLA Modules:
  0.0 57.5 jit_solution(7521247446703964092)
XLA Ops:
  0.0 56.2 %shard_map.64 = f32[32,256]{1,0:T(8,128)} custom-call(f32[96,256]{1,0:T(8,128)} %bitcast.6, f32[32,256]{1,0:T(8,128)} %charge_hbm.1, s32[27,256]{1,0:T(8,128)} %bitcast.7, s32[16,256]{1,0:T(8,128)} %bitcast.8, s32[8,128]{1,0:T(8,128)} %bitcast.9, f32[216,3456]{1,0:T(8,128)} %m2l_hbm.1), custom_call_target="tpu_custom_call" | custom-call | tf_op jit(solution)/shard_map/pallas_call | solution.py:431
  56.2 1.4 %copy.8 = f32[32,256]{1,0:T(8,128)} copy(f32[32,256]{1,0:T(8,128)} %shard_map.64) | data formatting | bytes 65536

commit v5 on v4

--- a/solution.py
+++ b/solution.py
@@ -268,18 +268,17 @@
     for move in moves:
         move.start()
 
-    def build(start):
+    def build(start, m):
         for part in range(2):
             at = pl.multiple_of(start + part * 64, 64)
             spread_tile(table[pl.ds(at, 64), :], spread, at)
-        moments_tile(table, spread, cells, moments, start)
+        moments_tile(table, spread, cells.at[m], moments.at[m], start)
 
     def build_row(first):
-        @pl.loop(0, 2)
-        def _(tile):
-            build(pl.multiple_of(first + tile * 128, 128))
-
-    moments[NODES:256, :] = jnp.zeros((256 - NODES, 128), F32)
+        for tile in range(2):
+            build(pl.multiple_of(first + tile * 128, 128), tile)
+
+    moments[:, NODES:256, :] = jnp.zeros((2, 256 - NODES, 128), F32)
     table[pl.ds(pl.multiple_of(own_first, OWN), OWN), :] = own[...]
     build_row(own_first)
 
@@ -331,9 +330,10 @@
         table[BESIDE + side * CAP : BESIDE + side * CAP + CAP, :] = beside[side]
     table[ZERO:TABLE, :] = jnp.zeros((TABLE - ZERO, 128), F32)
 
-    @pl.loop(ROW // 128, TABLE // 128)
-    def _(tile):
-        build(pl.multiple_of(tile * 128, 128))
+    @pl.loop(ROW // 256, TABLE // 256)
+    def _(pair):
+        for tile in range(2):
+            build(pl.multiple_of(pair * 256 + tile * 128, 128), tile)
 
     for move in moves:
         move.wait()
@@ -450,8 +450,8 @@
             pltpu.VMEM((FAR, 1, OWN), jnp.int32),
             pltpu.SMEM((NEAR * OWN,), jnp.int32),
             pltpu.SMEM((FAR * OWN,), jnp.int32),
-            pltpu.VMEM((128, 128), F32),
-            pltpu.VMEM((256, 128), F32),
+            pltpu.VMEM((2, 128, 128), F32),
+            pltpu.VMEM((2, 256, 128), F32),
             pltpu.VMEM((TABLE * 8, 128), F32),
             pltpu.VMEM((8 * OWN, 128), F32),
             pltpu.VMEM((FAR, OWN // 8, 16, 128), F32),

time: 57.7 us -> 57.4 us (level)
  no operation moved by 1% of the time
where the time goes in v5:
time: 57.4 us; the launch traced here: 57.2 us
  Pallas kernels  55.8 us (97%)
  local copies, waits for them, and re-layouts  1.38 us (2%)
    pallas_call x1, Pallas kernels, potential_call(): pl.pallas_call(potential_kernel, out_shape=jax.ShapeDtypeStruct((NB, OWN)...  55.8 us
    unnamed x1, local copies, waits for them, and re-layouts  1.38 us

profile of v5, /device:TPU:8, one launch (start us, length us, event | category | flops | bytes accessed | tf_op | source)
XLA Modules:
  0.0 57.2 jit_solution(17426339043346557973)
XLA Ops:
  0.0 55.8 %shard_map.64 = f32[32,256]{1,0:T(8,128)} custom-call(f32[96,256]{1,0:T(8,128)} %bitcast.6, f32[32,256]{1,0:T(8,128)} %charge_hbm.1, s32[27,256]{1,0:T(8,128)} %bitcast.7, s32[16,256]{1,0:T(8,128)} %bitcast.8, s32[8,128]{1,0:T(8,128)} %bitcast.9, f32[216,3456]{1,0:T(8,128)} %m2l_hbm.1), custom_call_target="tpu_custom_call" | custom-call | tf_op jit(solution)/shard_map/pallas_call | solution.py:431
  55.8 1.4 %copy.8 = f32[32,256]{1,0:T(8,128)} copy(f32[32,256]{1,0:T(8,128)} %shard_map.64) | data formatting | bytes 65536
